TPU v7x, 128 devices: a whole 4x4x4 slice. The times are simulated.
128 devices in a mesh: dp: 32 (over z, y, core), mp: 4 (over x).
Axes of the slice: x: 4, y: 4, z: 4, core: 2. Of those that a mesh axis runs over, the one named last changes fastest.
Arguments:
- patches: bfloat16 [49152, 128], P(('dp', 'mp')), may hold values from -6 to 6
- row_count: int32 [128], P(('dp', 'mp')), may hold values from 0 to 384, as said below
- target_group: int32 [49152], P(('dp', 'mp')), may hold values from 0 to 31, as said below
- target_offset: int32 [49152], P(('dp', 'mp')), may hold values from 0 to 639, as said below
- embed: bfloat16 [128, 6144], replicated, may hold values from -0.5 to 0.5
- norm_gain: bfloat16 [6144], replicated, may hold values from 0.099609375 to 1.8984375
- readout: bfloat16 [6144, 128], P('mp'), may hold values from -0.078125 to 0.078125
- target: bfloat16 [20480, 128], P('dp'), may hold values from -12 to 12
- master: float32 [6144, 6144], P('dp', 'mp'), may hold values from -6 to 6
- moment1: float32 [6144, 6144], P('dp', 'mp'), may hold values from -2 to 2
- moment2: float32 [6144, 6144], P('dp', 'mp'), may hold values from 0.0034722222 to 0.1388889
Outputs:
- prediction: float32 [20480, 128], P('dp')
- master_new: float32 [6144, 6144], P('dp', 'mp')
- moment1_new: float32 [6144, 6144], P('dp', 'mp')
- moment2_new: float32 [6144, 6144], P('dp', 'mp')
- weight_copy: bfloat16 [6144, 6144], P('dp', 'mp')
Inputs may be any that keep to these rules, and one draw needn't show every extreme that they name: Device i holds its live patch rows in its first row_count[i] slots; some device holds 384 of them in every draw. Over the live slots of all devices, each pair (target_group, target_offset) of the 20480 positions occurs exactly once; values in slots past row_count are arbitrary within the range. Call target_offset // 160 the block of a row. Each (batch, block) receives exactly 160 live rows; one device sends at most 3 live rows to one (batch, block), and every (batch, block) gets 3 rows from some device.
All inputs are finite; a program needn't handle non-finite values.
Results may differ from a plain program's by a relative error of at most 0.03.
Values may be sent and summed in bfloat16 or wider, within the bound.
A program may use at most 128 MiB of HBM per device.

v0:
```python
import jax
import jax.numpy as jnp
from jax import lax
from jax.sharding import PartitionSpec as P

gelu_const = 0.7978845608028654
beta_one = 0.9
beta_two = 0.95
learn_rate = 0.01
decay_rate = 0.1
adam_epsilon = 1e-08
step_count = 20


def gelu_tanh(value):
    inner = gelu_const * (value + 0.044715 * value * value * value)
    return 0.5 * value * (1.0 + jnp.tanh(inner))


def gelu_slope(value):
    tangent = jnp.tanh(gelu_const * (value + 0.044715 * value * value * value))
    return 0.5 * (1.0 + tangent) + 0.5 * value * (1.0 - tangent * tangent) * gelu_const * (
        1.0 + 3.0 * 0.044715 * value * value
    )


def shards(
    patches,
    row_count,
    target_group,
    target_offset,
    embed,
    norm_gain,
    readout,
    target,
    master,
    moment1,
    moment2,
):
    model_count = lax.axis_size("mp")
    batch_count = lax.axis_size("dp")
    devices_all = batch_count * model_count
    slot_total = patches.shape[0]
    capacity = slot_total // devices_all
    batch_rows = target.shape[0]
    block_rows = batch_rows // model_count
    width = embed.shape[1]
    patch_width = patches.shape[1]
    occupied = jnp.arange(slot_total, dtype=jnp.int32) < row_count[0]
    owner_index = jnp.where(
        occupied, target_group * model_count + target_offset // block_rows, devices_all
    )
    onehot = (owner_index[:, None] == jnp.arange(devices_all, dtype=jnp.int32)[None, :]).astype(
        jnp.int32
    )
    running = jnp.cumsum(onehot, axis=0)
    placing = jnp.sum(onehot * running, axis=1) - 1
    send_slot = jnp.where(occupied, owner_index * capacity + placing, devices_all * capacity)
    outgoing = (
        jnp.zeros((devices_all * capacity, patch_width), jnp.bfloat16)
        .at[send_slot]
        .set(patches, mode="drop")
    )
    slot_marks = (
        jnp.full((devices_all * capacity,), block_rows, jnp.int32)
        .at[send_slot]
        .set(target_offset % block_rows, mode="drop")
    )
    arrived, arrived_marks = (
        lax.all_to_all(outgoing, ("dp", "mp"), split_axis=0, concat_axis=0, tiled=True),
        lax.all_to_all(slot_marks, ("dp", "mp"), split_axis=0, concat_axis=0, tiled=True),
    )
    block_patches = (
        jnp.zeros((block_rows, patch_width), jnp.bfloat16)
        .at[arrived_marks]
        .set(arrived, mode="drop")
    )
    gain_wide = norm_gain.astype(jnp.float32)
    hidden = gelu_tanh(
        jnp.dot(
            lax.all_gather(block_patches, "mp", axis=0, tiled=True),
            embed,
            preferred_element_type=jnp.float32,
        )
    )
    normed = (
        hidden * lax.rsqrt(jnp.mean(hidden * hidden, axis=-1, keepdims=True) + 1e-05) * gain_wide
    ).astype(jnp.bfloat16)
    weight = master.astype(jnp.bfloat16)
    width_scale = 1.0 / width**0.5
    columns = normed
    preact = (
        jnp.dot(
            columns,
            lax.all_gather(weight, "dp", axis=0, tiled=True),
            preferred_element_type=jnp.float32,
        )
        * width_scale
    )
    activation = gelu_tanh(preact).astype(jnp.bfloat16)
    prediction = lax.psum(
        jnp.dot(activation, readout, preferred_element_type=jnp.float32).astype(jnp.bfloat16), "mp"
    ).astype(jnp.float32)
    errors = (prediction - target.astype(jnp.float32)).astype(jnp.bfloat16)
    backward = lax.dot_general(
        errors, readout, (((1,), (1,)), ((), ())), preferred_element_type=jnp.float32
    )
    delta_rows = (backward * gelu_slope(preact)).astype(jnp.bfloat16)
    columns = normed
    gradient = lax.psum_scatter(
        (
            lax.dot_general(
                columns, delta_rows, (((0,), (0,)), ((), ())), preferred_element_type=jnp.float32
            )
            * width_scale
        ).astype(jnp.bfloat16),
        "dp",
        scatter_dimension=0,
        tiled=True,
    ).astype(jnp.float32)
    moment1_new = beta_one * moment1 + (1.0 - beta_one) * gradient
    moment2_new = beta_two * moment2 + (1.0 - beta_two) * gradient * gradient
    first_fix = moment1_new / (1.0 - beta_one**step_count)
    second_fix = moment2_new / (1.0 - beta_two**step_count)
    master_new = master - learn_rate * (
        first_fix / (jnp.sqrt(second_fix) + adam_epsilon) + decay_rate * master
    )
    return (prediction, master_new, moment1_new, moment2_new, master_new.astype(jnp.bfloat16))


def solution(mesh):
    placed = (
        P(("dp", "mp"), None),
        P(("dp", "mp")),
        P(("dp", "mp")),
        P(("dp", "mp")),
        P(),
        P(),
        P("mp", None),
        P("dp", None),
        P("dp", "mp"),
        P("dp", "mp"),
        P("dp", "mp"),
    )
    return jax.shard_map(
        shards,
        mesh=mesh,
        in_specs=placed,
        out_specs=(P("dp", None), P("dp", "mp"), P("dp", "mp"), P("dp", "mp"), P("dp", "mp")),
        check_vma=False,
    )
```

profile of v0, /device:TPU:0, one launch (start us, length us, event | category | flops | bytes accessed | tf_op | source)
XLA Modules:
  0.0 316.7 jit_solution(15524870666545750787)
XLA Ops:
  7.2 0.0 copy-start
  7.2 0.0 copy-start.4
  7.2 0.0 all-gather.2.cloned.1.call-start
  7.2 2.3 convert_element_type.44
  9.5 0.0 all-gather.2.cloned.1.call-update
  10.2 0.7 add_select_fusion
  10.9 0.1 copy.18
  11.0 0.2 fusion.14
  11.3 0.1 broadcast_add_fusion
  11.3 0.2 fusion.16
  11.6 2.9 scatter_custom_fusion
  14.5 0.8 all_to_all.16
  15.3 11.1 %all-to-all-start = ((s32[128,3,1]{1,2,0:T(1,128)}), s32[128,3,1]{1,2,0:T(1,128)S(1)}, u32[]{:S(2)}, u32[]{:S(2)}) async-start(s32[128,3,1]{1,2,0:T(1,128)} %bitcast.5), calls=%async_computation | async-start | bytes 131072 | tf_op jit(solution)/shard_map/all_to_all | solution.py:71
  26.5 0.0 copy-done.4
  26.5 1.8 scatter_custom_fusion.1
  28.3 0.7 all_to_all.19
  29.0 6.7 %all-to-all-done = s32[128,3,1]{1,2,0:T(1,128)S(1)} async-done(((s32[128,3,1]{1,2,0:T(1,128)}), s32[128,3,1]{1,2,0:T(1,128)S(1)}, u32[]{:S(2)}, u32[]{:S(2)}) %all-to-all-start) | async-done | bytes 1568 | tf_op jit(solution)/shard_map/all_to_all | solution.py:71
  35.7 4.6 %all-to-all-start.1 = ((bf16[128,3,128]{2,1,0:T(4,128)(2,1)}), bf16[128,3,128]{2,1,0:T(4,128)(2,1)S(1)}, u32[]{:S(2)}, u32[]{:S(2)}) async-start(bf16[128,3,128]{2,1,0:T(4,128)(2,1)} %all_to_all.19), calls=%async_computation.1 | async-start | bytes 262144 | tf_op jit(solution)/shard_map/all_to_all | solution.py:70
  40.4 0.0 all-reduce.2.cloned.1.call-start
  40.4 0.5 broadcast.113
  40.9 0.8 reduce.5
  41.7 0.2 all_to_all.18
  42.0 7.9 %all-to-all-done.1 = bf16[128,3,128]{2,1,0:T(4,128)(2,1)S(1)} async-done(((bf16[128,3,128]{2,1,0:T(4,128)(2,1)}), bf16[128,3,128]{2,1,0:T(4,128)(2,1)S(1)}, u32[]{:S(2)}, u32[]{:S(2)}) %all-to-all-start.1) | async-done | bytes 98336 | tf_op jit(solution)/shard_map/all_to_all | solution.py:70
  49.8 0.1 reshape.88
  49.9 1.4 scatter_custom_fusion.2
  51.4 12.2 %all_gather.6 = bf16[640,128]{1,0:T(8,128)(2,1)S(1)} all-gather(bf16[160,128]{1,0:T(8,128)(2,1)S(1)} %scatter_custom_fusion.2), channel_id=1, replica_groups=mesh['dp'=32,'mp'=4] {'mp'}, dimensions={0}, use_global_device_ids=true | all-gather | bytes 204800 | tf_op jit(solution)/shard_map/all_gather | solution.py:81
  63.6 0.0 copy-done
  63.6 9.0 %multiply_reduce_fusion = (f32[640]{0:T(1024)S(1)}, f32[640,6144]{1,0:T(8,128)}) fusion(bf16[640,128]{1,0:T(8,128)(2,1)S(1)} %all_gather.6, bf16[128,6144]{1,0:T(8,128)(2,1)S(1)} %copy-done), kind=kOutput, calls=%fused_computation.10 | convolution fusion | flops 1045953920 | bytes 17467904 | tf_op jit(solution)/shard_map/dot_general | solution.py:80
  72.6 19.0 %all-gather.2.cloned.1.call-done = bf16[6144,1536]{1,0:T(8,128)(2,1)} async-done(((bf16[192,1536]{1,0:T(8,128)(2,1)}), bf16[6144,1536]{1,0:T(8,128)(2,1)}) %all-gather.2.cloned.1.call-update) | async-done | bytes 18874384 | tf_op jit(solution)/shard_map/all_gather | solution.py:95
  91.6 18.6 %fusion.40 = f32[640,1536]{1,0:T(8,128)S(1)} fusion(bf16[6144,1536]{1,0:T(8,128)(2,1)} %all-gather.2.cloned.1.call-done, f32[640,6144]{1,0:T(8,128)} %get-tuple-element.12, f32[6144]{0:T(1024)S(1)} %convert_element_type.42, f32[640]{0:T(1024)S(1)} %add_rsqrt_fusion), kind=kOutput, calls=%fused_computation.67 | convolution fusion | flops 12091392000 | bytes 38562304 | tf_op jit(solution)/shard_map/dot_general | solution.py:93
  110.2 0.0 copy-start.7
  110.2 2.0 copy-done.7
  112.2 0.0 copy-done.5
  112.2 2.2 fusion.13
  114.4 0.0 all-reduce.2.cloned.1.call-update
  114.4 0.3 reduce-scatter.2.cloned.1.call-start
  114.7 40.5 %all-reduce.2.cloned.1.call-done = bf16[640,128]{1,0:T(8,128)(2,1)} async-done(((bf16[640,128]{1,0:T(8,128)(2,1)}), bf16[640,128]{1,0:T(8,128)(2,1)}) %all-reduce.2.cloned.1.call-update) | async-done | bytes 163856 | tf_op jit(solution)/shard_map/psum | solution.py:101
  155.2 0.9 convert_element_type.47
  156.1 0.0 copy-done.6
  156.1 0.0 copy-start.3
  156.1 27.2 %multiply_convert_fusion = bf16[6144,1536]{1,0:T(8,128)(2,1)} fusion(f32[640,1536]{1,0:T(8,128)} %copy-done.7, bf16[1536,128]{1,0:T(8,128)(2,1)S(1)} %copy-done.5, f32[640,128]{1,0:T(8,128)S(1)} %convert_element_type.47, bf16[640,128]{1,0:T(8,128)(2,1)S(1)} %copy-done.6, f32[640,6144]{1,0:T(8,128)} %get-tuple-element.12, f32[6144]{0:T(1024)S(1)} %convert_element_type.42, ...), kind=kOutput, calls=%fused_computation.3 | convolution fusion | flops 12381831168 | bytes 39447040 | tf_op jit(solution)/shard_map/dot_general | solution.py:112
  183.4 0.0 copy-done.3
  183.4 0.0 reduce-scatter.2.cloned.1.call-update
  183.4 0.0 copy-start.1
  183.4 122.3 %reduce-scatter.2.cloned.1.call-done = bf16[192,1536]{1,0:T(8,128)(2,1)} async-done(((bf16[6144,1536]{1,0:T(8,128)(2,1)}), bf16[192,1536]{1,0:T(8,128)(2,1)}) %reduce-scatter.2.cloned.1.call-update) | async-done | bytes 589840 | tf_op jit(solution)/shard_map/reduce_scatter | solution.py:110
  305.7 0.0 copy-done.2
  305.7 4.4 %fusion.41 = (bf16[192,1536]{1,0:T(8,128)(2,1)}, f32[192,1536]{1,0:T(8,128)}, f32[192,1536]{1,0:T(8,128)}, f32[192,1536]{1,0:T(8,128)}) fusion(f32[192,1536]{1,0:T(8,128)S(1)} %copy-done.2, bf16[192,1536]{1,0:T(8,128)(2,1)} %reduce-scatter.2.cloned.1.call-done, f32[192,1536]{1,0:T(8,128)} %param.20, f32[192,1536]{1,0:T(8,128)} %param.21), kind=kLoop, calls=%fused_computation.68 | loop fusion | flops 5013504 | bytes 8257536 | tf_op jit(solution)/shard_map/convert_element_type | solution.py:128
  310.1 0.0 copy-done.1
  (10 shorter events, 0.1 us)
Async XLA Ops:
  7.2 56.4 %copy-start = (bf16[128,6144]{1,0:T(8,128)(2,1)S(1)}, bf16[128,6144]{1,0:T(8,128)(2,1)}, u32[]{:S(2)}) copy-start(bf16[128,6144]{1,0:T(8,128)(2,1)} %param.15) | copy-start | bytes 4718596
  7.2 19.3 %copy-start.4 = (bf16[6144]{0:T(1024)(128)(2,1)S(1)}, bf16[6144]{0:T(1024)(128)(2,1)}, u32[]{:S(2)}) copy-start(bf16[6144]{0:T(1024)(128)(2,1)} %param.16) | copy-start | bytes 36868
  7.2 84.4 %all-gather.2.cloned.1.call-start = ((), (), s32[]{:S(2)}) async-start(), calls=%async_computation.3 | async-start | bytes 19464192 | tf_op jit(solution)/shard_map/all_gather | solution.py:95
  15.3 20.4 %all-to-all-start = ((s32[128,3,1]{1,2,0:T(1,128)}), s32[128,3,1]{1,2,0:T(1,128)S(1)}, u32[]{:S(2)}, u32[]{:S(2)}) async-start(s32[128,3,1]{1,2,0:T(1,128)} %bitcast.5), calls=%async_computation | async-start | bytes 131072 | tf_op jit(solution)/shard_map/all_to_all | solution.py:71
  35.7 14.1 %all-to-all-start.1 = ((bf16[128,3,128]{2,1,0:T(4,128)(2,1)}), bf16[128,3,128]{2,1,0:T(4,128)(2,1)S(1)}, u32[]{:S(2)}, u32[]{:S(2)}) async-start(bf16[128,3,128]{2,1,0:T(4,128)(2,1)} %all_to_all.19), calls=%async_computation.1 | async-start | bytes 262144 | tf_op jit(solution)/shard_map/all_to_all | solution.py:70
  40.4 114.8 %all-reduce.2.cloned.1.call-start = ((), (), s32[]{:S(2)}) async-start(), calls=%async_computation.4 | async-start | bytes 327680 | tf_op jit(solution)/shard_map/psum | solution.py:101
  91.6 20.6 %copy-start.5 = (bf16[1536,128]{1,0:T(8,128)(2,1)S(1)}, bf16[1536,128]{1,0:T(8,128)(2,1)}, u32[]{:S(2)}) copy-start(bf16[1536,128]{1,0:T(8,128)(2,1)} %param.17) | copy-start | bytes 1179652
  110.2 2.0 copy-start.7
  112.2 43.9 %copy-start.6 = (bf16[640,128]{1,0:T(8,128)(2,1)S(1)}, bf16[640,128]{1,0:T(8,128)(2,1)}, u32[]{:S(2)}) copy-start(bf16[640,128]{1,0:T(8,128)(2,1)} %param.18) | copy-start | bytes 491524
  114.4 191.3 %reduce-scatter.2.cloned.1.call-start = ((), (), s32[]{:S(2)}) async-start(), calls=%async_computation.5 | async-start | bytes 19464192 | tf_op jit(solution)/shard_map/reduce_scatter | solution.py:110
  156.1 27.3 %copy-start.3 = (f32[640,128]{1,0:T(8,128)}, f32[640,128]{1,0:T(8,128)S(1)}, u32[]{:S(2)}) copy-start(f32[640,128]{1,0:T(8,128)S(1)} %convert_element_type.47) | copy-start | bytes 983044
  183.4 122.3 %copy-start.2 = (f32[192,1536]{1,0:T(8,128)S(1)}, f32[192,1536]{1,0:T(8,128)}, u32[]{:S(2)}) copy-start(f32[192,1536]{1,0:T(8,128)} %param.19) | copy-start | bytes 3538948
  183.4 126.7 %copy-start.1 = (bf16[128,6144]{1,0:T(8,128)(2,1)S(1)}, bf16[128,6144]{1,0:T(8,128)(2,1)}, u32[]{:S(2)}) copy-start(bf16[128,6144]{1,0:T(8,128)(2,1)} %param.15) | copy-start | bytes 4718596
Sparse Core Ops, SparseCore 0:
  10.9 80.6 all-gather.1
  114.5 40.6 all-reduce.1
  183.5 122.1 reduce-scatter.1
where the time goes:
time: 317 us
  waiting for transfers between devices  196 us (62%)
  matrix products  57 us (18%)
  starting transfers between devices  16.1 us (5%)
  between operations  14.6 us (5%)
  blocking collectives  12.2 us (4%)
  local copies, waits for them, and re-layouts  10.7 us (3%)
  other arithmetic  9.67 us (3%)
    reduce_scatter x1, waiting for transfers between devices, shards(): lax.psum_scatter((lax.dot_general(columns, delta_rows, (((0,), (0,)), (()...  122 us
    psum x1, waiting for transfers between devices, shards(): lax.psum(jnp.dot(activation, readout, preferred_element_type=jnp.float32)...  40.5 us
    dot_general x1, matrix products, shards(): lax.dot_general(columns, delta_rows, (((0,), (0,)), ((), ())), preferred_...  27.2 us
    all_gather x1, waiting for transfers between devices, shards(): lax.all_gather(weight, 'dp', axis=0, tiled=True)  19 us
    dot_general x1, matrix products, shards(): jnp.dot(columns, lax.all_gather(weight, 'dp', axis=0, tiled=True), prefer...  18.6 us
    all_gather x1, blocking collectives, shards(): lax.all_gather(block_patches, 'mp', axis=0, tiled=True)  12.2 us
    all_to_all x1, starting transfers between devices, shards(): lax.all_to_all(slot_marks, ('dp', 'mp'), split_axis=0, concat_axis=0, til...  11.1 us
    dot_general x1, matrix products, shards(): jnp.dot(lax.all_gather(block_patches, 'mp', axis=0, tiled=True), embed, p...  8.99 us
  transfers between devices with their start and end apart: 5, of which 5 were waited for; matrix products, arithmetic and copies ran while one was open for 6% of the time, Pallas kernels for 0%

commit v1 on v0

--- a/solution.py
+++ b/solution.py
@@ -98,8 +98,12 @@
         * width_scale
     )
     activation = gelu_tanh(preact).astype(jnp.bfloat16)
-    prediction = lax.psum(
-        jnp.dot(activation, readout, preferred_element_type=jnp.float32).astype(jnp.bfloat16), "mp"
+    prediction = jnp.sum(
+        lax.all_gather(
+            jnp.dot(activation, readout, preferred_element_type=jnp.float32).astype(jnp.bfloat16),
+            "mp",
+        ),
+        axis=0,
     ).astype(jnp.float32)
     errors = (prediction - target.astype(jnp.float32)).astype(jnp.bfloat16)
     backward = lax.dot_general(

time: 317 us -> 286 us (0.902)
  waiting for transfers between devices: 196 us -> 155 us
  blocking collectives: 12.2 us -> 26 us
    psum x1 -> x0, waiting for transfers between devices: 40.5 us -> none  [shards(): lax.psum(jnp.dot(activation, readout, preferred_element_type=jnp.float32)...]
    all_gather x0 -> x1, blocking collectives: none -> 13.7 us  [shards(): lax.all_gather(jnp.dot(activation, readout, preferred_element_type=jnp.fl...]
  transfers between devices with their start and end apart: 5 -> 4, of which waited for: 5 -> 4; matrix products, arithmetic and copies ran while one was open for 6% -> 6% of each run, Pallas kernels for 0% -> 0%
where the time goes in v1:
time: 286 us
  waiting for transfers between devices  155 us (54%)
  matrix products  56.4 us (20%)
  blocking collectives  26 us (9%)
  starting transfers between devices  15.9 us (6%)
  between operations  14.9 us (5%)
  local copies, waits for them, and re-layouts  9.17 us (3%)
  other arithmetic  8.88 us (3%)
    reduce_scatter x1, waiting for transfers between devices, shards(): lax.psum_scatter((lax.dot_general(columns, delta_rows, (((0,), (0,)), (()...  121 us
    dot_general x1, matrix products, shards(): lax.dot_general(columns, delta_rows, (((0,), (0,)), ((), ())), preferred_...  27.3 us
    all_gather x1, waiting for transfers between devices, shards(): lax.all_gather(weight, 'dp', axis=0, tiled=True)  19 us
    dot_general x1, matrix products, shards(): jnp.dot(columns, lax.all_gather(weight, 'dp', axis=0, tiled=True), prefer...  18.6 us
    all_gather x1, blocking collectives, shards(): lax.all_gather(jnp.dot(activation, readout, preferred_element_type=jnp.fl...  13.7 us
    all_gather x1, blocking collectives, shards(): lax.all_gather(block_patches, 'mp', axis=0, tiled=True)  12.2 us
    all_to_all x1, starting transfers between devices, shards(): lax.all_to_all(slot_marks, ('dp', 'mp'), split_axis=0, concat_axis=0, til...  11.1 us
    dot_general x1, matrix products, shards(): jnp.dot(lax.all_gather(block_patches, 'mp', axis=0, tiled=True), embed, p...  8.99 us
  transfers between devices with their start and end apart: 4, of which 4 were waited for; matrix products, arithmetic and copies ran while one was open for 6% of the time, Pallas kernels for 0%

profile of v1, /device:TPU:0, one launch (start us, length us, event | category | flops | bytes accessed | tf_op | source)
XLA Modules:
  0.0 286.1 jit_solution(13497228313792468630)
XLA Ops:
  7.2 0.0 copy-start
  7.2 0.0 copy-start.4
  7.2 0.0 all-gather.3.cloned.1.call-start
  7.2 2.3 convert_element_type.46
  9.5 0.0 all-gather.3.cloned.1.call-update
  10.2 0.7 add_select_fusion
  10.9 0.1 copy.18
  11.0 0.2 fusion.14
  11.3 0.1 broadcast_add_fusion
  11.3 0.2 fusion.16
  11.6 2.9 %scatter_custom_fusion = s32[384]{0:T(512)S(1)} fusion(s32[384]{0:T(512)S(1)} %compare_select_fusion.1, s32[384]{0:T(512)S(1)} %get-tuple-element.9, s32[]{:T(128)} %constant.29.clone.1), kind=kCustom, calls=%fused_computation.53 | custom fusion | bytes 1540 | tf_op jit(solution)/shard_map/scatter | solution.py:67
  14.5 0.8 all_to_all.16
  15.3 11.1 %all-to-all-start = ((s32[128,3,1]{1,2,0:T(1,128)}), s32[128,3,1]{1,2,0:T(1,128)S(1)}, u32[]{:S(2)}, u32[]{:S(2)}) async-start(s32[128,3,1]{1,2,0:T(1,128)} %bitcast.5), calls=%async_computation | async-start | bytes 131072 | tf_op jit(solution)/shard_map/all_to_all | solution.py:71
  26.5 0.0 copy-done.4
  26.5 1.8 scatter_custom_fusion.1
  28.3 0.7 all_to_all.19
  29.0 6.7 %all-to-all-done = s32[128,3,1]{1,2,0:T(1,128)S(1)} async-done(((s32[128,3,1]{1,2,0:T(1,128)}), s32[128,3,1]{1,2,0:T(1,128)S(1)}, u32[]{:S(2)}, u32[]{:S(2)}) %all-to-all-start) | async-done | bytes 1568 | tf_op jit(solution)/shard_map/all_to_all | solution.py:71
  35.7 4.6 %all-to-all-start.1 = ((bf16[128,3,128]{2,1,0:T(4,128)(2,1)}), bf16[128,3,128]{2,1,0:T(4,128)(2,1)S(1)}, u32[]{:S(2)}, u32[]{:S(2)}) async-start(bf16[128,3,128]{2,1,0:T(4,128)(2,1)} %all_to_all.19), calls=%async_computation.1 | async-start | bytes 262144 | tf_op jit(solution)/shard_map/all_to_all | solution.py:70
  40.4 0.0 reduce-scatter.2.cloned.1.call-start
  40.4 0.5 broadcast.113
  40.9 0.8 reduce.6
  41.7 0.2 all_to_all.18
  42.0 7.9 %all-to-all-done.1 = bf16[128,3,128]{2,1,0:T(4,128)(2,1)S(1)} async-done(((bf16[128,3,128]{2,1,0:T(4,128)(2,1)}), bf16[128,3,128]{2,1,0:T(4,128)(2,1)S(1)}, u32[]{:S(2)}, u32[]{:S(2)}) %all-to-all-start.1) | async-done | bytes 98336 | tf_op jit(solution)/shard_map/all_to_all | solution.py:70
  49.8 0.1 reshape.88
  49.9 1.4 scatter_custom_fusion.2
  51.4 12.2 %all_gather.12 = bf16[640,128]{1,0:T(8,128)(2,1)S(1)} all-gather(bf16[160,128]{1,0:T(8,128)(2,1)S(1)} %scatter_custom_fusion.2), channel_id=1, replica_groups=mesh['dp'=32,'mp'=4] {'mp'}, dimensions={0}, use_global_device_ids=true | all-gather | bytes 204800 | tf_op jit(solution)/shard_map/all_gather | solution.py:81
  63.6 0.0 copy-done
  63.6 9.0 %multiply_reduce_fusion = (f32[640]{0:T(1024)S(1)}, f32[640,6144]{1,0:T(8,128)}) fusion(bf16[640,128]{1,0:T(8,128)(2,1)S(1)} %all_gather.12, bf16[128,6144]{1,0:T(8,128)(2,1)S(1)} %copy-done), kind=kOutput, calls=%fused_computation.10 | convolution fusion | flops 1045953920 | bytes 17467904 | tf_op jit(solution)/shard_map/dot_general | solution.py:80
  72.6 19.0 %all-gather.3.cloned.1.call-done = bf16[6144,1536]{1,0:T(8,128)(2,1)} async-done(((bf16[192,1536]{1,0:T(8,128)(2,1)}), bf16[6144,1536]{1,0:T(8,128)(2,1)}) %all-gather.3.cloned.1.call-update) | async-done | bytes 18874384 | tf_op jit(solution)/shard_map/all_gather | solution.py:95
  91.6 0.0 copy-start.5
  91.6 18.6 %fusion.40 = f32[640,1536]{1,0:T(8,128)S(1)} fusion(bf16[6144,1536]{1,0:T(8,128)(2,1)} %all-gather.3.cloned.1.call-done, f32[640,6144]{1,0:T(8,128)} %get-tuple-element.12, f32[6144]{0:T(1024)S(1)} %convert_element_type.44, f32[640]{0:T(1024)S(1)} %add_rsqrt_fusion), kind=kOutput, calls=%fused_computation.67 | convolution fusion | flops 12091392000 | bytes 38562304 | tf_op jit(solution)/shard_map/dot_general | solution.py:93
  110.2 0.0 copy-done.5
  110.2 0.0 copy-start.7
  110.2 0.0 copy-start.6
  110.2 1.5 fusion.13
  111.7 0.5 copy-done.7
  112.2 13.7 %all-gather = bf16[2560,128]{1,0:T(8,128)(2,1)S(1)} all-gather(bf16[640,128]{1,0:T(8,128)(2,1)S(1)} %fusion.13), channel_id=2, replica_groups=mesh['dp'=32,'mp'=4] {'mp'}, dimensions={0}, use_global_device_ids=true | all-gather | bytes 819200 | tf_op jit(solution)/shard_map/all_gather | solution.py:102
  125.9 0.1 reduce_sum.32
  126.1 0.0 copy-done.6
  126.1 0.0 copy-start.3
  126.1 27.3 %multiply_convert_fusion = bf16[6144,1536]{1,0:T(8,128)(2,1)} fusion(f32[640,1536]{1,0:T(8,128)} %copy-done.7, bf16[1536,128]{1,0:T(8,128)(2,1)S(1)} %copy-done.5, f32[640,128]{1,0:T(8,128)S(1)} %convert_element_type.49, bf16[640,128]{1,0:T(8,128)(2,1)S(1)} %copy-done.6, f32[640,6144]{1,0:T(8,128)} %get-tuple-element.12, f32[6144]{0:T(1024)S(1)} %convert_element_type.44, ...), kind=kOutput, calls=%fused_computation.3 | convolution fusion | flops 12381831168 | bytes 39447040 | tf_op jit(solution)/shard_map/dot_general | solution.py:116
  153.4 0.0 copy-done.3
  153.4 0.0 reduce-scatter.2.cloned.1.call-update
  153.4 0.0 copy-start.1
  153.4 121.5 %reduce-scatter.2.cloned.1.call-done = bf16[192,1536]{1,0:T(8,128)(2,1)} async-done(((bf16[6144,1536]{1,0:T(8,128)(2,1)}), bf16[192,1536]{1,0:T(8,128)(2,1)}) %reduce-scatter.2.cloned.1.call-update) | async-done | bytes 589840 | tf_op jit(solution)/shard_map/reduce_scatter | solution.py:114
  274.9 0.0 copy-done.2
  274.9 4.4 %fusion.41 = (bf16[192,1536]{1,0:T(8,128)(2,1)}, f32[192,1536]{1,0:T(8,128)}, f32[192,1536]{1,0:T(8,128)}, f32[192,1536]{1,0:T(8,128)}) fusion(f32[192,1536]{1,0:T(8,128)S(1)} %copy-done.2, bf16[192,1536]{1,0:T(8,128)(2,1)} %reduce-scatter.2.cloned.1.call-done, f32[192,1536]{1,0:T(8,128)} %param.20, f32[192,1536]{1,0:T(8,128)} %param.21), kind=kLoop, calls=%fused_computation.68 | loop fusion | flops 5013504 | bytes 8257536 | tf_op jit(solution)/shard_map/convert_element_type | solution.py:132
  279.3 0.0 copy-done.1
  (9 shorter events, 0.1 us)
Async XLA Ops:
  7.2 56.4 %copy-start = (bf16[128,6144]{1,0:T(8,128)(2,1)S(1)}, bf16[128,6144]{1,0:T(8,128)(2,1)}, u32[]{:S(2)}) copy-start(bf16[128,6144]{1,0:T(8,128)(2,1)} %param.15) | copy-start | bytes 4718596
  7.2 19.3 %copy-start.4 = (bf16[6144]{0:T(1024)(128)(2,1)S(1)}, bf16[6144]{0:T(1024)(128)(2,1)}, u32[]{:S(2)}) copy-start(bf16[6144]{0:T(1024)(128)(2,1)} %param.16) | copy-start | bytes 36868
  7.2 84.4 %all-gather.3.cloned.1.call-start = ((), (), s32[]{:S(2)}) async-start(), calls=%async_computation.3 | async-start | bytes 19464192 | tf_op jit(solution)/shard_map/all_gather | solution.py:95
  15.3 20.4 %all-to-all-start = ((s32[128,3,1]{1,2,0:T(1,128)}), s32[128,3,1]{1,2,0:T(1,128)S(1)}, u32[]{:S(2)}, u32[]{:S(2)}) async-start(s32[128,3,1]{1,2,0:T(1,128)} %bitcast.5), calls=%async_computation | async-start | bytes 131072 | tf_op jit(solution)/shard_map/all_to_all | solution.py:71
  35.7 14.1 %all-to-all-start.1 = ((bf16[128,3,128]{2,1,0:T(4,128)(2,1)}), bf16[128,3,128]{2,1,0:T(4,128)(2,1)S(1)}, u32[]{:S(2)}, u32[]{:S(2)}) async-start(bf16[128,3,128]{2,1,0:T(4,128)(2,1)} %all_to_all.19), calls=%async_computation.1 | async-start | bytes 262144 | tf_op jit(solution)/shard_map/all_to_all | solution.py:70
  40.4 234.5 %reduce-scatter.2.cloned.1.call-start = ((), (), s32[]{:S(2)}) async-start(), calls=%async_computation.4 | async-start | bytes 19464192 | tf_op jit(solution)/shard_map/reduce_scatter | solution.py:114
  91.6 18.6 %copy-start.5 = (bf16[1536,128]{1,0:T(8,128)(2,1)S(1)}, bf16[1536,128]{1,0:T(8,128)(2,1)}, u32[]{:S(2)}) copy-start(bf16[1536,128]{1,0:T(8,128)(2,1)} %param.17) | copy-start | bytes 1179652
  110.2 2.0 copy-start.7
  110.2 15.9 %copy-start.6 = (bf16[640,128]{1,0:T(8,128)(2,1)S(1)}, bf16[640,128]{1,0:T(8,128)(2,1)}, u32[]{:S(2)}) copy-start(bf16[640,128]{1,0:T(8,128)(2,1)} %param.18) | copy-start | bytes 491524
  126.1 27.3 %copy-start.3 = (f32[640,128]{1,0:T(8,128)}, f32[640,128]{1,0:T(8,128)S(1)}, u32[]{:S(2)}) copy-start(f32[640,128]{1,0:T(8,128)S(1)} %convert_element_type.49) | copy-start | bytes 983044
  153.4 121.5 %copy-start.2 = (f32[192,1536]{1,0:T(8,128)S(1)}, f32[192,1536]{1,0:T(8,128)}, u32[]{:S(2)}) copy-start(f32[192,1536]{1,0:T(8,128)} %param.19) | copy-start | bytes 3538948
  153.4 125.9 %copy-start.1 = (bf16[128,6144]{1,0:T(8,128)(2,1)S(1)}, bf16[128,6144]{1,0:T(8,128)(2,1)}, u32[]{:S(2)}) copy-start(bf16[128,6144]{1,0:T(8,128)(2,1)} %param.15) | copy-start | bytes 4718596
Sparse Core Ops, SparseCore 0:
  10.9 80.6 all-gather.2
  153.5 121.3 reduce-scatter.1
